TPU v7x, 256 devices: a whole 4x4x8 slice. The times are simulated.
256 devices in a mesh: tok: 64 (over y, z, core), feat: 4 (over x).
Axes of the slice: x: 4, y: 4, z: 8, core: 2. Of those that a mesh axis runs over, the one named last changes fastest.
Arguments:
- activations: bfloat16 [16384, 16384], P('tok', 'feat'), may hold values from -0.0625 to 0.0625
- targets: float32 [16384, 32], P('tok'), may hold values from -6 to 6
- counts: int32 [64], P('tok'), may hold values from 1 to 256, 8192 in all
- ridge: float32 [32], replicated, may hold values from 0.1 to 1
Outputs:
- weights: float32 [16384, 32], P('feat')
- residual: float32 [16384, 32], P('tok')
Inputs may be any that keep to these rules, and one draw needn't show every extreme that they name: The counts of all shards sum to 8192.
All inputs are finite; a program needn't handle non-finite values.
Results may differ from a plain program's by a relative error of at most 0.033.
Values may be sent and summed in bfloat16 or wider, within the bound.
A program may use at most 64 MiB of HBM per device.

v0:
```python
import jax
import jax.numpy as jnp
from jax import lax
from jax.sharding import PartitionSpec as P

ITERS = 4


def local(activations, targets, counts, ridge):
    rows = activations.shape[0]
    tok_size = lax.axis_size("tok")
    feat_size = lax.axis_size("feat")
    count = counts[0]
    live = (jnp.arange(rows, dtype=jnp.int32) < count).astype(jnp.float32)[:, None]

    def backward(resid_bf):
        dims = (((0,), (0,)), ((), ()))
        return lax.dot_general(activations, resid_bf, dims, preferred_element_type=jnp.float32)

    def gradient_of(resid, weights):
        partial_cols = backward(resid.astype(jnp.bfloat16))
        summed = lax.psum(partial_cols, "tok")
        grad = summed - ridge[None, :] * weights
        gamma = lax.psum(jnp.sum(grad * grad, axis=0), "feat")
        return (grad, gamma)

    residual = targets * live
    share_rows = activations.shape[1]
    norm_scale = 1.0 / tok_size
    weights = jnp.zeros((share_rows, targets.shape[1]), jnp.float32)
    grad, gamma = gradient_of(residual, weights)
    direction = grad
    for step in range(ITERS):
        direct_bf = direction.astype(jnp.bfloat16)
        partial_rows = jnp.dot(activations, direct_bf, preferred_element_type=jnp.float32)
        image = lax.psum(partial_rows.astype(jnp.bfloat16), "feat").astype(jnp.float32) * live
        local_terms = (
            jnp.sum(image * image, axis=0) / feat_size
            + ridge * jnp.sum(direction * direction, axis=0) * norm_scale
        )
        delta = lax.psum(local_terms, ("tok", "feat"))
        alpha = gamma / delta
        weights = weights + alpha[None, :] * direction
        residual = residual - alpha[None, :] * image
        if step + 1 < ITERS:
            grad, gamma_new = gradient_of(residual, weights)
            direction = grad + (gamma_new / gamma)[None, :] * direction
            gamma = gamma_new
    return (weights, residual)


def solution(mesh):
    placed = (P("tok", "feat"), P("tok", None), P("tok"), P())
    return jax.shard_map(
        local,
        mesh=mesh,
        in_specs=placed,
        out_specs=(P("feat", None), P("tok", None)),
        check_vma=False,
    )
```

profile of v0, /device:TPU:1, one launch (start us, length us, event | category | flops | bytes accessed | tf_op | source)
XLA Modules:
  0.0 1147.2 jit_solution(1337250138402758811)
XLA Ops:
  7.2 0.0 copy-start
  7.2 0.0 copy-start.5
  7.2 0.0 all-reduce.5.cloned.1.call-start
  8.0 0.7 copy-done
  8.8 2.0 convolution_bitcast_fusion.3
  10.8 0.0 copy-start.4
  10.8 0.0 all-reduce.5.cloned.1.call-update
  10.8 0.0 all-reduce.7.cloned.1.call-start
  10.9 0.0 copy-done.5
  10.9 184.3 %all-reduce.5.cloned.1.call-done = f32[4096,32]{0,1:T(8,128)} async-done(((f32[4096,32]{0,1:T(8,128)}), f32[4096,32]{0,1:T(8,128)}) %all-reduce.5.cloned.1.call-update) | async-done | bytes 524304 | tf_op jit(solution)/shard_map/psum | solution.py:22
  195.2 0.0 copy-start.1
  195.2 1.8 fusion
  197.0 13.2 %psum.114 = bf16[256,32]{0,1:T(8,128)(2,1)S(1)} all-reduce(bf16[256,32]{0,1:T(8,128)(2,1)S(1)} %fusion), channel_id=1, replica_groups=mesh['tok'=64,'feat'=4] {'feat'}, use_global_device_ids=true, to_apply=%region_3.0 | all-reduce | flops 8192 | bytes 32768 | tf_op jit(solution)/shard_map/psum | solution.py:36
  210.2 0.1 multiply_reduce_fusion.10
  210.3 0.0 copy-done.1
  210.3 0.2 multiply_reduce_fusion.6
  210.6 6.0 psum.113
  216.6 80.6 %psum.115 = f32[32]{0:T(128)S(1)} all-reduce(f32[32]{0:T(128)S(1)} %multiply_add_fusion.9), channel_id=1, replica_groups=mesh['tok'=64,'feat'=4] {'tok','feat'}, use_global_device_ids=true, to_apply=%region_5.0 | all-reduce | flops 32 | bytes 256 | tf_op jit(solution)/shard_map/psum | solution.py:41
  297.2 0.0 copy-done.4
  297.2 1.3 convolution_bitcast_fusion.2
  298.5 0.0 all-reduce.7.cloned.1.call-update
  298.6 0.0 all-reduce.9.cloned.1.call-start
  298.6 174.9 %all-reduce.7.cloned.1.call-done = f32[4096,32]{0,1:T(8,128)} async-done(((f32[4096,32]{0,1:T(8,128)}), f32[4096,32]{0,1:T(8,128)}) %all-reduce.7.cloned.1.call-update) | async-done | bytes 524304 | tf_op jit(solution)/shard_map/psum | solution.py:22
  473.5 1.3 multiply_reduce_fusion.5
  474.9 8.5 psum.117
  483.4 1.4 multiply_reduce_fusion.4
  484.7 0.0 copy-start.2
  484.7 0.8 copy-done.2
  485.5 0.7 fusion.1
  486.3 11.0 psum.118
  497.2 0.1 multiply_reduce_fusion.9
  497.4 79.8 %psum.119 = f32[32]{0:T(128)S(1)} all-reduce(f32[32]{0:T(128)S(1)} %multiply_add_fusion.8), channel_id=1, replica_groups=mesh['tok'=64,'feat'=4] {'tok','feat'}, use_global_device_ids=true, to_apply=%region_12.0 | all-reduce | flops 32 | bytes 256 | tf_op jit(solution)/shard_map/psum | solution.py:41
  577.2 1.3 convolution_bitcast_fusion.1
  578.5 0.0 all-reduce.9.cloned.1.call-update
  578.5 0.0 all-reduce.11.cloned.1.call-start
  578.6 175.7 %all-reduce.9.cloned.1.call-done = f32[4096,32]{0,1:T(8,128)} async-done(((f32[4096,32]{0,1:T(8,128)}), f32[4096,32]{0,1:T(8,128)}) %all-reduce.9.cloned.1.call-update) | async-done | bytes 524304 | tf_op jit(solution)/shard_map/psum | solution.py:22
  754.2 1.5 multiply_reduce_fusion.3
  755.7 8.5 psum.121
  764.2 1.5 multiply_reduce_fusion.2
  765.7 0.7 fusion.2
  766.5 11.0 psum.122
  777.4 0.1 multiply_reduce_fusion.8
  777.6 79.8 %psum.123 = f32[32]{0:T(128)S(1)} all-reduce(f32[32]{0:T(128)S(1)} %multiply_add_fusion.7), channel_id=1, replica_groups=mesh['tok'=64,'feat'=4] {'tok','feat'}, use_global_device_ids=true, to_apply=%region_19.0 | all-reduce | flops 32 | bytes 256 | tf_op jit(solution)/shard_map/psum | solution.py:41
  857.4 1.3 convolution_bitcast_fusion
  858.7 0.0 all-reduce.11.cloned.1.call-update
  858.7 175.7 %all-reduce.11.cloned.1.call-done = f32[4096,32]{0,1:T(8,128)} async-done(((f32[4096,32]{0,1:T(8,128)}), f32[4096,32]{0,1:T(8,128)}) %all-reduce.11.cloned.1.call-update) | async-done | bytes 524304 | tf_op jit(solution)/shard_map/psum | solution.py:22
  1034.4 1.3 multiply_reduce_fusion.1
  1035.7 8.5 psum.125
  1044.2 1.4 multiply_reduce_fusion
  1045.6 0.0 copy-start.3
  1045.6 0.8 copy-done.3
  1046.4 0.7 fusion.3
  1047.1 11.0 psum.126
  1058.1 0.1 multiply_reduce_fusion.7
  1058.2 79.8 %psum.127 = f32[32]{0:T(128)S(1)} all-reduce(f32[32]{0:T(128)S(1)} %multiply_add_fusion.6), channel_id=1, replica_groups=mesh['tok'=64,'feat'=4] {'tok','feat'}, use_global_device_ids=true, to_apply=%region_26.0 | all-reduce | flops 32 | bytes 256 | tf_op jit(solution)/shard_map/psum | solution.py:41
  1138.0 0.7 multiply_subtract_fusion.3
  1138.7 2.0 multiply_add_fusion
  (13 shorter events, 0.1 us)
Async XLA Ops:
  7.2 1.6 copy-start
  7.2 3.7 copy-start.5
  7.2 188.0 %all-reduce.5.cloned.1.call-start = ((), (), s32[]{:S(2)}) async-start(), calls=%async_computation | async-start | bytes 1048576 | tf_op jit(solution)/shard_map/psum | solution.py:22
  10.8 286.4 %copy-start.4 = (f32[256,32]{0,1:T(8,128)S(1)}, f32[256,32]{0,1:T(8,128)}, u32[]{:S(2)}) copy-start(f32[256,32]{0,1:T(8,128)} %param.5) | copy-start | bytes 98308
  10.8 462.7 %all-reduce.7.cloned.1.call-start = ((), (), s32[]{:S(2)}) async-start(), calls=%async_computation.1 | async-start | bytes 1048576 | tf_op jit(solution)/shard_map/psum | solution.py:22
  195.2 15.1 %copy-start.1 = (f32[4096,32]{0,1:T(8,128)S(1)}, f32[4096,32]{0,1:T(8,128)}, u32[]{:S(2)}) copy-start(f32[4096,32]{0,1:T(8,128)} %all-reduce.5.cloned.1.call-done) | copy-start | bytes 1572868
  298.6 455.7 %all-reduce.9.cloned.1.call-start = ((), (), s32[]{:S(2)}) async-start(), calls=%async_computation.2 | async-start | bytes 1048576 | tf_op jit(solution)/shard_map/psum | solution.py:22
  484.7 0.8 copy-start.2
  578.5 455.9 %all-reduce.11.cloned.1.call-start = ((), (), s32[]{:S(2)}) async-start(), calls=%async_computation.3 | async-start | bytes 1048576 | tf_op jit(solution)/shard_map/psum | solution.py:22
  1045.6 0.8 copy-start.3
Sparse Core Ops, SparseCore 0:
  12.1 183.0 all-reduce.4
  298.7 174.8 all-reduce.6
  578.6 175.5 all-reduce.8
  858.8 175.5 all-reduce.10
where the time goes:
time: 1150 us
  waiting for transfers between devices  711 us (62%)
  blocking collectives  398 us (35%)
  between operations  14.6 us (1%)
  other arithmetic  11.8 us (1%)
    psum x4, waiting for transfers between devices, gradient_of(): summed = lax.psum(partial_cols, 'tok')  711 us
    psum x4, blocking collectives, local(): delta = lax.psum(local_terms, ('tok', 'feat'))  320 us
    psum x4, blocking collectives, local(): lax.psum(partial_rows.astype(jnp.bfloat16), 'feat').astype(jnp.float32)  46.1 us
    psum x4, blocking collectives, gradient_of(): gamma = lax.psum(jnp.sum(grad * grad, axis=0), 'feat')  31.5 us
  transfers between devices with their start and end apart: 4, of which 4 were waited for; matrix products, arithmetic and copies ran while one was open for 0% of the time, Pallas kernels for 0%

commit v1 on v0

v1 whole, which is shorter than its diff:
```python
import jax
import jax.numpy as jnp
from jax import lax
from jax.experimental import pallas as pl
from jax.experimental.pallas import tpu as pltpu
from jax.sharding import PartitionSpec as P

ITERS = 4
NY, NZ, NX = 4, 8, 4
CHIPS = NY * NZ
MESH = pl.DeviceIdType.MESH
F32, BF16 = jnp.float32, jnp.bfloat16


def hops(offset):
    dy, dz = offset
    return min(dy, NY - dy) + min(dz, NZ - dz)


OFFSETS = sorted(((dy, dz) for dy in range(NY) for dz in range(NZ)), key=lambda o: (-hops(o), o))
PEERS = CHIPS - 1
GROUPS = ((0, 5), (5, 12), (12, 20), (20, 32))
TILE = 128


def kernel(a_hbm, y_ref, count_ref, ridge_ref, w_out, p_out, r_out, q_out, alpha_out,
           a, ysend, yrecv, mask, r, q, s, p, w, total, tsend, trecv, drow, g, xbuf, xrow, alpha_buf,
           load_sem, push_send, push_recv, y_sems, t_send, t_recv, d_send, d_recv,
           g_send, g_recv, x_send, x_recv, xr_send, xr_recv, pub_local, pub_send, pub_recv):
    tok, x = lax.axis_index("tok"), lax.axis_index("feat")
    core = lax.rem(tok, 2)
    z, y = lax.rem(tok // 2, NZ), tok // (2 * NZ)
    chips = [lax.rem(y + dy, NY) * NZ + lax.rem(z + dz, NZ) for dy, dz in OFFSETS]
    me = chips[-1]
    mine = pl.ds(pl.multiple_of(core * 256, 256), 256)
    others = pl.ds(pl.multiple_of((1 - core) * 256, 256), 256)
    sibling = (me * 2 + 1 - core, x)
    peers = [(chip * 2 + core, x) for chip in chips[:PEERS]]
    x_peers = [(tok, lax.rem(x + d, NX)) for d in (2, 1, 3)]

    def tile(chip):
        return pl.ds(pl.multiple_of(chip * TILE, TILE), TILE)

    def slots(lo, hi):
        return slice(lo * TILE, hi * TILE)

    def send(src, dst, send_sem, recv_sem, device):
        copy = pltpu.make_async_remote_copy(
            src_ref=src, dst_ref=dst, send_sem=send_sem, recv_sem=recv_sem,
            device_id=device, device_id_type=MESH)
        copy.start()
        return copy

    def wait(ref, sem):
        pltpu.make_async_copy(ref, ref, sem).wait()

    for group, (lo, hi) in enumerate(GROUPS):
        for j in range(lo, hi):
            pltpu.make_async_copy(
                a_hbm.at[:, tile(chips[j])], a.at[mine, slots(j, j + 1)], load_sem.at[group]).start()

    barrier = pltpu.get_barrier_semaphore()
    for device in peers + x_peers + [sibling]:
        pl.semaphore_signal(barrier, inc=1, device_id=device, device_id_type=MESH)

    live = (lax.broadcasted_iota(jnp.int32, (32, 256), 1) < count_ref[0]).astype(F32)
    own_rows = pl.ds(pl.multiple_of(core * 16, 16), 16)
    sibling_rows = pl.ds(pl.multiple_of((1 - core) * 16, 16), 16)
    ysend[0:16, :] = y_ref[sibling_rows, :] * live[0:16]
    ysend[16:24, :] = live[0:8]
    r[:, mine] = y_ref[own_rows, :] * live[0:16]
    mask[:, mine] = live[0:8]
    q[...] = jnp.zeros_like(q)
    p[...] = jnp.zeros_like(p)
    w[...] = jnp.zeros_like(w)
    total[...] = jnp.zeros_like(total)

    lane = lax.broadcasted_iota(jnp.int32, (16, TILE), 1)
    sub = lax.broadcasted_iota(jnp.int32, (16, TILE), 0)
    eye = (lane == sub).astype(F32)
    eye2 = (lane == sub + 16).astype(F32)
    pick = (lax.broadcasted_iota(jnp.int32, (16, 32), 1)
            == lax.broadcasted_iota(jnp.int32, (16, 32), 0) + core * 16).astype(F32)
    ridge = jnp.sum(ridge_ref[...] * pick, axis=1, keepdims=True)

    def to_row(column, which):
        return jnp.sum(column * which, axis=0, keepdims=True)

    def to_column(row, which):
        return jnp.sum(row * which, axis=1, keepdims=True)

    def lanes(v):
        out = v[:, 0:TILE]
        for j in range(1, v.shape[1] // TILE):
            out = out + v[:, j * TILE:(j + 1) * TILE]
        return jnp.sum(out, axis=1, keepdims=True)

    def curvature(n):
        wait(drow.at[n, pl.ds(0, PEERS)], d_recv.at[n])
        row = drow[n, 0]
        for j in range(1, CHIPS):
            row = row + drow[n, j]
        return to_column(row, eye)

    def send_row(n, j):
        send(drow.at[n, me], drow.at[n, me], d_send, d_recv.at[n], peers[j])

    pl.semaphore_wait(barrier, PEERS + NX)

    y_copy = send(ysend, yrecv, y_sems.at[0], y_sems.at[1], sibling)
    pushes = []
    for group, (lo, hi) in enumerate(GROUPS):
        wait(a.at[mine, slots(lo, hi)], load_sem.at[group])
        part = a.at[mine, slots(lo, hi)]
        pushes.append(send(part, part, push_send.at[group], push_recv.at[group], sibling))
    y_copy.wait()
    r[:, others] = yrecv[0:16, :]
    mask[:, others] = yrecv[16:24, :]
    s[...] = r[...].astype(BF16)
    drow[0, me] = to_row(lanes(r[...] * r[...]), eye)

    def step(n, carry):
        gamma, norm, guess, beta = carry
        for group, (lo, hi) in enumerate(GROUPS):
            @pl.when(n == 0)
            def _():
                pushes[group].wait_recv()
            part = jnp.dot(s[...], a[:, slots(lo, hi)], preferred_element_type=F32)
            tsend[n, :, slots(lo, hi)] = part.astype(BF16)
            for j in range(lo, min(hi, PEERS)):
                send(tsend.at[n, :, slots(j, j + 1)], trecv.at[n, j], t_send, t_recv.at[n, group], peers[j])
                send_row(n, j)
            if hi == CHIPS:
                summed = part[:, (PEERS - lo) * TILE:]

        @pl.when(n > 0)
        def _():
            p[...] = g[n - 1].astype(F32) + beta * p[...]

        for group, (lo, hi) in reversed(list(enumerate(GROUPS))):
            hi = min(hi, PEERS)
            wait(trecv.at[n, pl.ds(lo, hi - lo)], t_recv.at[n, group])
            for j in range(lo, hi):
                summed = summed + trecv[n, j].astype(F32)
        energy = curvature(n)
        first = n == 0
        alpha = jnp.where(first, 0.0, gamma / (energy + ridge * norm))
        ratio = jnp.where(first, 1.0, alpha / guess)
        fresh = (1.0 - ratio) * total[...] + ratio * summed
        total[...] = fresh
        g[n, :, tile(me)] = (fresh - ridge * (w[:, tile(me)] + alpha * p[:, tile(me)])).astype(BF16)
        for group, (lo, hi) in enumerate(GROUPS):
            for j in range(lo, min(hi, PEERS)):
                part = g.at[n, :, tile(me)]
                send(part, part, g_send, g_recv.at[n, group], peers[j])
        r[...] = r[...] - alpha * q[...]
        w[...] = w[...] + alpha * p[...]

        image = jnp.zeros((16, 512), F32)
        for group, (lo, hi) in reversed(list(enumerate(GROUPS))):
            wait(g.at[n, :, slots(0, min(hi, PEERS) - lo)], g_recv.at[n, group])
            for j in reversed(range(lo, hi)):
                image = image + lax.dot_general(
                    g[n, :, tile(chips[j])], a[:, slots(j, j + 1)], (((1,), (1,)), ((), ())),
                    preferred_element_type=F32)
        xbuf[n, x] = image.astype(BF16)
        for device in x_peers:
            send(xbuf.at[n, x], xbuf.at[n, x], x_send, x_recv.at[n], device)
        grad = g[n].astype(F32)
        xrow[n, x] = to_row(lanes(grad * grad), eye) + to_row(lanes(grad * p[...]), eye2)
        for device in x_peers:
            send(xrow.at[n, x], xrow.at[n, x], xr_send, xr_recv.at[n], device)
        wait(xrow.at[n, pl.ds(0, NX - 1)], xr_recv.at[n])
        row = (xrow[n, 0] + xrow[n, 1]) + (xrow[n, 2] + xrow[n, 3])
        gamma_new = to_column(row, eye)
        cross = to_column(row, eye2)
        beta = jnp.where(first, 0.0, gamma_new / gamma)
        norm = gamma_new + 2.0 * beta * cross + beta * beta * norm
        guess = jnp.where(first, (2.0 / 3.0) * energy / gamma_new, 1.15 * alpha)
        wait(xbuf.at[n, pl.ds(0, NX - 1)], x_recv.at[n])
        image = ((xbuf[n, 0].astype(F32) + xbuf[n, 1].astype(F32))
                 + (xbuf[n, 2].astype(F32) + xbuf[n, 3].astype(F32)))
        fresh_q = image * mask[0:1, :] + beta * q[...]
        q[...] = fresh_q
        s[...] = (r[...] - guess * fresh_q).astype(BF16)
        drow[n + 1, me] = to_row(lanes(fresh_q * fresh_q), eye)
        return gamma_new, norm, guess, beta

    one = jnp.ones((16, 1), F32)
    gamma, norm, guess, beta = lax.fori_loop(0, ITERS, step, (one, one, one, one))

    for j in range(PEERS):
        send_row(ITERS, j)

    def publish(k, here, there, out):
        pltpu.make_async_copy(here, out.at[own_rows], pub_local.at[k]).start()
        send(there, out.at[own_rows], pub_send.at[k], pub_recv.at[k], sibling)

    publish(0, w, w, w_out)
    publish(1, r.at[:, mine], r.at[:, others], r_out)
    publish(2, q.at[:, mine], q.at[:, others], q_out)
    p[...] = g[ITERS - 1].astype(F32) + beta * p[...]
    publish(3, p, p, p_out)
    alpha = gamma / (curvature(ITERS) + ridge * norm)
    alpha_buf[...] = jnp.broadcast_to(alpha, alpha_buf.shape)
    publish(4, alpha_buf, alpha_buf, alpha_out)
    for k, (src, out) in enumerate(((w, w_out), (r.at[:, mine], r_out), (q.at[:, mine], q_out),
                                    (p, p_out), (alpha_buf, alpha_out))):
        wait(src, pub_local.at[k])
        wait(src, pub_send.at[k])
        wait(out.at[sibling_rows], pub_recv.at[k])
    for push in pushes:
        push.wait_send()
    wait(tsend.at[:, :, slots(0, PEERS)], t_send)
    wait(g.at[:, :, slots(0, PEERS)], g_send)
    wait(drow.at[:, pl.ds(0, PEERS)], d_send)
    wait(xbuf.at[:, pl.ds(0, NX - 1)], x_send)
    wait(xrow.at[:, pl.ds(0, NX - 1)], xr_send)


def local(activations, targets, counts, ridge):
    any_ = pl.BlockSpec(memory_space=pl.ANY)
    vmem = pl.BlockSpec(memory_space=pltpu.VMEM)
    dma = pltpu.SemaphoreType.DMA
    groups = len(GROUPS)
    w, p, r, q, alpha = pl.pallas_call(
        kernel,
        out_shape=[jax.ShapeDtypeStruct((32, n), F32) for n in (4096, 4096, 256, 256, TILE)],
        in_specs=[any_, vmem, pl.BlockSpec(memory_space=pltpu.SMEM), vmem],
        out_specs=[any_] * 5,
        scratch_shapes=[
            pltpu.VMEM((512, 4096), BF16),
            pltpu.VMEM((24, 256), F32),
            pltpu.VMEM((24, 256), F32),
            pltpu.VMEM((8, 512), F32),
            pltpu.VMEM((16, 512), F32),
            pltpu.VMEM((16, 512), F32),
            pltpu.VMEM((16, 512), BF16),
            pltpu.VMEM((16, 4096), F32),
            pltpu.VMEM((16, 4096), F32),
            pltpu.VMEM((16, TILE), F32),
            pltpu.VMEM((ITERS, 16, 4096), BF16),
            pltpu.VMEM((ITERS, PEERS, 16, TILE), BF16),
            pltpu.VMEM((ITERS + 1, CHIPS, 1, TILE), F32),
            pltpu.VMEM((ITERS, 16, 4096), BF16),
            pltpu.VMEM((ITERS, NX, 16, 512), BF16),
            pltpu.VMEM((ITERS, NX, 1, TILE), F32),
            pltpu.VMEM((16, TILE), F32),
            dma((groups,)), dma((groups,)), dma((groups,)), dma((2,)),
            dma, dma((ITERS, groups)), dma, dma((ITERS + 1,)),
            dma, dma((ITERS, groups)), dma, dma((ITERS,)), dma, dma((ITERS,)),
            dma((5,)), dma((5,)), dma((5,)),
        ],
        compiler_params=pltpu.CompilerParams(
            collective_id=0, has_side_effects=True, vmem_limit_bytes=40 * 2**20),
        name="cgls",
    )(activations, targets.T, counts, ridge[None, :])
    step = alpha[:, 0:1]
    return (w + step * p).T, (r - step * q).T


def solution(mesh):
    placed = (P("tok", "feat"), P("tok", None), P("tok"), P())
    return jax.shard_map(
        local,
        mesh=mesh,
        in_specs=placed,
        out_specs=(P("feat", None), P("tok", None)),
        check_vma=False,
    )
```

time: 1150 us -> 97 us (0.08)
  waiting for transfers between devices: 711 us -> 0 us
  blocking collectives: 398 us -> 0 us
  Pallas kernels: 0 us -> 90.8 us
  between operations: 14.6 us -> 1.3 us
    psum x4 -> x0, waiting for transfers between devices: 711 us -> none  [gradient_of(): summed = lax.psum(partial_cols, 'tok')]
    psum x12 -> x0, blocking collectives: 398 us -> none  [the longest x4 320 us: local(): delta = lax.psum(local_terms, ('tok', 'feat'))]
    pallas_call x0 -> x1, Pallas kernels: none -> 90.8 us  [local(): pl.pallas_call(kernel, out_shape=[jax.ShapeDtypeStruct((32, n), F32) for...]
  transfers between devices with their start and end apart: 4 -> 0, of which waited for: 4 -> 0; matrix products, arithmetic and copies ran while one was open for 0% -> 0% of each run, Pallas kernels for 0% -> 0%
where the time goes in v1:
time: 97 us; the launch traced here: 96.8 us
  Pallas kernels  90.8 us (94%)
  local copies, waits for them, and re-layouts  3.11 us (3%)
  other arithmetic  1.61 us (2%)
  between operations  1.3 us (1%)
    pallas_call x1, Pallas kernels, local(): pl.pallas_call(kernel, out_shape=[jax.ShapeDtypeStruct((32, n), F32) for...  90.8 us
    unnamed x6, local copies, waits for them, and re-layouts  3 us

profile of v1, /device:TPU:1, one launch (start us, length us, event | category | flops | bytes accessed | tf_op | source)
XLA Modules:
  0.0 96.8 jit_solution(2397794342244301794)
XLA Ops:
  1.3 0.0 copy-start
  1.3 1.6 %copy-done = bf16[256,4096]{1,0:T(8,128)(2,1)S(1)} copy-done((bf16[256,4096]{1,0:T(8,128)(2,1)S(1)}, bf16[256,4096]{1,0:T(8,128)(2,1)}, u32[]{:S(2)}) %copy-start) | copy-done | bytes 2097176
  2.9 0.0 copy-start.1
  2.9 0.8 copy-done.1
  3.6 0.0 copy-start.2
  3.6 0.7 copy-done.2
  4.3 90.8 %cgls.1 = (f32[32,4096]{1,0:T(8,128)S(1)}, f32[32,4096]{1,0:T(8,128)S(1)}, f32[32,256]{1,0:T(8,128)S(1)}, f32[32,256]{1,0:T(8,128)S(1)}, f32[32,128]{1,0:T(8,128)S(1)}) custom-call(bf16[256,4096]{1,0:T(8,128)(2,1)S(1)} %copy-done, f32[32,256]{1,0:T(8,128)S(1)} %bitcast.6, s32[1]{0:T(128)S(6)} %copy.6.count_ref, f32[1,32]{1,0:T(1,128)S(1)} %bitcast.7), custom_call_target="tpu_custom_call" | custom-call | tf_op jit(solution)/shard_map/cgls/pallas_call | solution.py:226
  95.1 0.1 slice_reduce_fusion
  95.2 0.7 subtract_bitcast_fusion
  95.9 0.9 add_bitcast_fusion
Async XLA Ops:
  1.3 1.6 %copy-start = (bf16[256,4096]{1,0:T(8,128)(2,1)S(1)}, bf16[256,4096]{1,0:T(8,128)(2,1)}, u32[]{:S(2)}) copy-start(bf16[256,4096]{1,0:T(8,128)(2,1)} %a_hbm.1) | copy-start | bytes 6291460
  2.9 0.8 copy-start.1
  3.6 0.7 copy-start.2

commit v2 on v1

--- a/solution.py
+++ b/solution.py
@@ -19,14 +19,14 @@
 
 OFFSETS = sorted(((dy, dz) for dy in range(NY) for dz in range(NZ)), key=lambda o: (-hops(o), o))
 PEERS = CHIPS - 1
-GROUPS = ((0, 5), (5, 12), (12, 20), (20, 32))
+GROUPS = ((0, 1), (1, 5), (5, 12), (12, 20), (20, 27), (27, 32))
 TILE = 128
 
 
-def kernel(a_hbm, y_ref, count_ref, ridge_ref, w_out, p_out, r_out, q_out, alpha_out,
-           a, ysend, yrecv, mask, r, q, s, p, w, total, tsend, trecv, drow, g, xbuf, xrow, alpha_buf,
+def kernel(a_hbm, y_hbm, count_hbm, ridge_hbm, w_out, p_out, r_out, q_out, alpha_out,
+           y_ref, count_ref, ridge_ref, in_sems, a, at, ysend, yrecv, mask, r, q, s, p, w, total, tsend, trecv, drow, ahead, g, xbuf, alpha_buf,
            load_sem, push_send, push_recv, y_sems, t_send, t_recv, d_send, d_recv,
-           g_send, g_recv, x_send, x_recv, xr_send, xr_recv, pub_local, pub_send, pub_recv):
+           g_send, g_recv, x_send, x_recv, pub_local, pub_send, pub_recv):
     tok, x = lax.axis_index("tok"), lax.axis_index("feat")
     core = lax.rem(tok, 2)
     z, y = lax.rem(tok // 2, NZ), tok // (2 * NZ)
@@ -54,15 +54,22 @@
     def wait(ref, sem):
         pltpu.make_async_copy(ref, ref, sem).wait()
 
+    barrier = pltpu.get_barrier_semaphore()
+    for device in peers + x_peers + [sibling]:
+        pl.semaphore_signal(barrier, inc=1, device_id=device, device_id_type=MESH)
+
+    inputs = [
+        pltpu.make_async_copy(src, dst, in_sems.at[k])
+        for k, (src, dst) in enumerate(((count_hbm, count_ref), (y_hbm, y_ref), (ridge_hbm, ridge_ref)))]
+    for copy in inputs:
+        copy.start()
     for group, (lo, hi) in enumerate(GROUPS):
         for j in range(lo, hi):
             pltpu.make_async_copy(
                 a_hbm.at[:, tile(chips[j])], a.at[mine, slots(j, j + 1)], load_sem.at[group]).start()
 
-    barrier = pltpu.get_barrier_semaphore()
-    for device in peers + x_peers + [sibling]:
-        pl.semaphore_signal(barrier, inc=1, device_id=device, device_id_type=MESH)
-
+    for copy in inputs:
+        copy.wait()
     live = (lax.broadcasted_iota(jnp.int32, (32, 256), 1) < count_ref[0]).astype(F32)
     own_rows = pl.ds(pl.multiple_of(core * 16, 16), 16)
     sibling_rows = pl.ds(pl.multiple_of((1 - core) * 16, 16), 16)
@@ -78,7 +85,7 @@
     lane = lax.broadcasted_iota(jnp.int32, (16, TILE), 1)
     sub = lax.broadcasted_iota(jnp.int32, (16, TILE), 0)
     eye = (lane == sub).astype(F32)
-    eye2 = (lane == sub + 16).astype(F32)
+    field = lane // 16
     pick = (lax.broadcasted_iota(jnp.int32, (16, 32), 1)
             == lax.broadcasted_iota(jnp.int32, (16, 32), 0) + core * 16).astype(F32)
     ridge = jnp.sum(ridge_ref[...] * pick, axis=1, keepdims=True)
@@ -94,6 +101,18 @@
         for j in range(1, v.shape[1] // TILE):
             out = out + v[:, j * TILE:(j + 1) * TILE]
         return jnp.sum(out, axis=1, keepdims=True)
+
+    def pack(*columns):
+        out = jnp.zeros((16, TILE), F32)
+        for k, column in enumerate(columns):
+            for place in range(3):
+                head = column.astype(BF16).astype(F32)
+                out = jnp.where(field == 3 * k + place, head, out)
+                column = column - head
+        return out.astype(BF16)
+
+    def unpack(v):
+        return [jnp.sum(jnp.where(field // 3 == k, v, 0.0), axis=1, keepdims=True) * 0.0625 for k in range(2)]
 
     def curvature(n):
         wait(drow.at[n, pl.ds(0, PEERS)], d_recv.at[n])
@@ -121,6 +140,8 @@
 
     def step(n, carry):
         gamma, norm, guess, beta = carry
+        first = n == 0
+        inv_gamma, inv_guess = 1.0 / gamma, 1.0 / guess
         for group, (lo, hi) in enumerate(GROUPS):
             @pl.when(n == 0)
             def _():
@@ -129,58 +150,62 @@
             tsend[n, :, slots(lo, hi)] = part.astype(BF16)
             for j in range(lo, min(hi, PEERS)):
                 send(tsend.at[n, :, slots(j, j + 1)], trecv.at[n, j], t_send, t_recv.at[n, group], peers[j])
-                send_row(n, j)
             if hi == CHIPS:
                 summed = part[:, (PEERS - lo) * TILE:]
+        for j in range(PEERS):
+            send_row(n, j)
+
+        @pl.when(n == 0)
+        def _():
+            for lo, hi in GROUPS:
+                at[slots(lo, hi), :] = a[:, slots(lo, hi)].T
 
         @pl.when(n > 0)
         def _():
-            p[...] = g[n - 1].astype(F32) + beta * p[...]
-
+            p[...] = g[...].astype(F32) + beta * p[...]
+
+        summed = summed - ridge * (w[:, tile(me)] + guess * p[:, tile(me)])
         for group, (lo, hi) in reversed(list(enumerate(GROUPS))):
             hi = min(hi, PEERS)
             wait(trecv.at[n, pl.ds(lo, hi - lo)], t_recv.at[n, group])
             for j in range(lo, hi):
                 summed = summed + trecv[n, j].astype(F32)
-        energy = curvature(n)
-        first = n == 0
-        alpha = jnp.where(first, 0.0, gamma / (energy + ridge * norm))
-        ratio = jnp.where(first, 1.0, alpha / guess)
-        fresh = (1.0 - ratio) * total[...] + ratio * summed
-        total[...] = fresh
-        g[n, :, tile(me)] = (fresh - ridge * (w[:, tile(me)] + alpha * p[:, tile(me)])).astype(BF16)
+        ahead[n, :, tile(me)] = summed.astype(BF16)
         for group, (lo, hi) in enumerate(GROUPS):
             for j in range(lo, min(hi, PEERS)):
-                part = g.at[n, :, tile(me)]
+                part = ahead.at[n, :, tile(me)]
                 send(part, part, g_send, g_recv.at[n, group], peers[j])
+
+        energy = curvature(n)
+        alpha = jnp.where(first, 0.0, gamma / (energy + ridge * norm))
+        ratio = jnp.where(first, 1.0, alpha * inv_guess)
         r[...] = r[...] - alpha * q[...]
         w[...] = w[...] + alpha * p[...]
+        total[...] = (1.0 - ratio) * total[...]
 
         image = jnp.zeros((16, 512), F32)
         for group, (lo, hi) in reversed(list(enumerate(GROUPS))):
-            wait(g.at[n, :, slots(0, min(hi, PEERS) - lo)], g_recv.at[n, group])
+            wait(ahead.at[n, :, slots(0, min(hi, PEERS) - lo)], g_recv.at[n, group])
             for j in reversed(range(lo, hi)):
-                image = image + lax.dot_general(
-                    g[n, :, tile(chips[j])], a[:, slots(j, j + 1)], (((1,), (1,)), ((), ())),
-                    preferred_element_type=F32)
-        xbuf[n, x] = image.astype(BF16)
+                at_j = tile(chips[j])
+                grad = total[:, at_j] + ratio * ahead[n, :, at_j].astype(F32)
+                total[:, at_j] = grad
+                grad = grad.astype(BF16)
+                g[:, at_j] = grad
+                image = image + jnp.dot(grad, at[slots(j, j + 1), :], preferred_element_type=F32)
+        grad = g[...].astype(F32)
+        xbuf[n, x, :, 512:] = pack(lanes(grad * grad), lanes(grad * p[...]))
+        xbuf[n, x, :, 0:512] = image.astype(BF16)
         for device in x_peers:
             send(xbuf.at[n, x], xbuf.at[n, x], x_send, x_recv.at[n], device)
-        grad = g[n].astype(F32)
-        xrow[n, x] = to_row(lanes(grad * grad), eye) + to_row(lanes(grad * p[...]), eye2)
-        for device in x_peers:
-            send(xrow.at[n, x], xrow.at[n, x], xr_send, xr_recv.at[n], device)
-        wait(xrow.at[n, pl.ds(0, NX - 1)], xr_recv.at[n])
-        row = (xrow[n, 0] + xrow[n, 1]) + (xrow[n, 2] + xrow[n, 3])
-        gamma_new = to_column(row, eye)
-        cross = to_column(row, eye2)
-        beta = jnp.where(first, 0.0, gamma_new / gamma)
-        norm = gamma_new + 2.0 * beta * cross + beta * beta * norm
-        guess = jnp.where(first, (2.0 / 3.0) * energy / gamma_new, 1.15 * alpha)
         wait(xbuf.at[n, pl.ds(0, NX - 1)], x_recv.at[n])
         image = ((xbuf[n, 0].astype(F32) + xbuf[n, 1].astype(F32))
                  + (xbuf[n, 2].astype(F32) + xbuf[n, 3].astype(F32)))
-        fresh_q = image * mask[0:1, :] + beta * q[...]
+        gamma_new, cross = unpack(image[:, 512:])
+        beta = jnp.where(first, 0.0, gamma_new * inv_gamma)
+        norm = gamma_new + 2.0 * beta * cross + beta * beta * norm
+        guess = jnp.where(first, (2.0 / 3.0) * energy / gamma_new, 1.15 * alpha)
+        fresh_q = image[:, 0:512] * mask[0:1, :] + beta * q[...]
         q[...] = fresh_q
         s[...] = (r[...] - guess * fresh_q).astype(BF16)
         drow[n + 1, me] = to_row(lanes(fresh_q * fresh_q), eye)
@@ -199,7 +224,7 @@
     publish(0, w, w, w_out)
     publish(1, r.at[:, mine], r.at[:, others], r_out)
     publish(2, q.at[:, mine], q.at[:, others], q_out)
-    p[...] = g[ITERS - 1].astype(F32) + beta * p[...]
+    p[...] = g[...].astype(F32) + beta * p[...]
     publish(3, p, p, p_out)
     alpha = gamma / (curvature(ITERS) + ridge * norm)
     alpha_buf[...] = jnp.broadcast_to(alpha, alpha_buf.shape)
@@ -212,24 +237,59 @@
     for push in pushes:
         push.wait_send()
     wait(tsend.at[:, :, slots(0, PEERS)], t_send)
-    wait(g.at[:, :, slots(0, PEERS)], g_send)
+    wait(ahead.at[:, :, slots(0, PEERS)], g_send)
     wait(drow.at[:, pl.ds(0, PEERS)], d_send)
     wait(xbuf.at[:, pl.ds(0, NX - 1)], x_send)
-    wait(xrow.at[:, pl.ds(0, NX - 1)], xr_send)
+
+
+PARTS = 4
+
+
+def finish(w_hbm, p_hbm, r_hbm, q_hbm, alpha_hbm, w_out, r_out, w, p, r, q, alpha, in_sems, out_sems):
+    width = w.shape[1] // PARTS
+    parts = [(slice(None), slice(k * width, (k + 1) * width)) for k in range(PARTS)]
+    small = [
+        pltpu.make_async_copy(src, dst, in_sems.at[k])
+        for k, (src, dst) in enumerate(((alpha_hbm, alpha), (r_hbm, r), (q_hbm, q)))]
+    large = [
+        pltpu.make_async_copy(src.at[part], dst.at[part], in_sems.at[3 + 2 * k + which])
+        for k, part in enumerate(parts) for which, (src, dst) in enumerate(((w_hbm, w), (p_hbm, p)))]
+    for copy in small + large:
+        copy.start()
+    for copy in small:
+        copy.wait()
+    step = alpha[:, 0:1]
+    r[...] = r[...] - step * q[...]
+    stores = [pltpu.make_async_copy(r, r_out, out_sems.at[PARTS])]
+    stores[0].start()
+    for k, part in enumerate(parts):
+        large[2 * k].wait()
+        large[2 * k + 1].wait()
+        w[part] = w[part] + step * p[part]
+        store = pltpu.make_async_copy(w.at[part], w_out.at[part], out_sems.at[k])
+        store.start()
+        stores.append(store)
+    for store in stores:
+        store.wait()
 
 
 def local(activations, targets, counts, ridge):
     any_ = pl.BlockSpec(memory_space=pl.ANY)
-    vmem = pl.BlockSpec(memory_space=pltpu.VMEM)
+    hbm = pl.BlockSpec(memory_space=pltpu.HBM)
     dma = pltpu.SemaphoreType.DMA
     groups = len(GROUPS)
     w, p, r, q, alpha = pl.pallas_call(
         kernel,
         out_shape=[jax.ShapeDtypeStruct((32, n), F32) for n in (4096, 4096, 256, 256, TILE)],
-        in_specs=[any_, vmem, pl.BlockSpec(memory_space=pltpu.SMEM), vmem],
+        in_specs=[hbm] * 4,
         out_specs=[any_] * 5,
         scratch_shapes=[
+            pltpu.VMEM((32, 256), F32),
+            pltpu.SMEM((1,), jnp.int32),
+            pltpu.VMEM((1, 32), F32),
+            dma((3,)),
             pltpu.VMEM((512, 4096), BF16),
+            pltpu.VMEM((4096, 512), BF16),
             pltpu.VMEM((24, 256), F32),
             pltpu.VMEM((24, 256), F32),
             pltpu.VMEM((8, 512), F32),
@@ -238,25 +298,37 @@
             pltpu.VMEM((16, 512), BF16),
             pltpu.VMEM((16, 4096), F32),
             pltpu.VMEM((16, 4096), F32),
-            pltpu.VMEM((16, TILE), F32),
+            pltpu.VMEM((16, 4096), F32),
             pltpu.VMEM((ITERS, 16, 4096), BF16),
             pltpu.VMEM((ITERS, PEERS, 16, TILE), BF16),
             pltpu.VMEM((ITERS + 1, CHIPS, 1, TILE), F32),
             pltpu.VMEM((ITERS, 16, 4096), BF16),
-            pltpu.VMEM((ITERS, NX, 16, 512), BF16),
-            pltpu.VMEM((ITERS, NX, 1, TILE), F32),
+            pltpu.VMEM((16, 4096), BF16),
+            pltpu.VMEM((ITERS, NX, 16, 512 + TILE), BF16),
             pltpu.VMEM((16, TILE), F32),
             dma((groups,)), dma((groups,)), dma((groups,)), dma((2,)),
             dma, dma((ITERS, groups)), dma, dma((ITERS + 1,)),
-            dma, dma((ITERS, groups)), dma, dma((ITERS,)), dma, dma((ITERS,)),
+            dma, dma((ITERS, groups)), dma, dma((ITERS,)),
             dma((5,)), dma((5,)), dma((5,)),
         ],
         compiler_params=pltpu.CompilerParams(
-            collective_id=0, has_side_effects=True, vmem_limit_bytes=40 * 2**20),
+            collective_id=0, has_side_effects=True, vmem_limit_bytes=58 * 2**20),
         name="cgls",
     )(activations, targets.T, counts, ridge[None, :])
-    step = alpha[:, 0:1]
-    return (w + step * p).T, (r - step * q).T
+    w, r = pl.pallas_call(
+        finish,
+        out_shape=[jax.ShapeDtypeStruct((32, n), F32) for n in (4096, 256)],
+        in_specs=[hbm] * 5,
+        out_specs=[any_] * 2,
+        scratch_shapes=[
+            pltpu.VMEM((32, 4096), F32), pltpu.VMEM((32, 4096), F32),
+            pltpu.VMEM((32, 256), F32), pltpu.VMEM((32, 256), F32), pltpu.VMEM((32, TILE), F32),
+            dma((2 * PARTS + 3,)), dma((PARTS + 1,)),
+        ],
+        compiler_params=pltpu.CompilerParams(vmem_limit_bytes=58 * 2**20),
+        name="finish",
+    )(w, p, r, q, alpha)
+    return w.T, r.T
 
 
 def solution(mesh):

time: 97 us -> 91.7 us (0.945)
  local copies, waits for them, and re-layouts: 3.11 us -> 0 us
  other arithmetic: 1.61 us -> 0 us
    unnamed x6 -> x0, local copies, waits for them, and re-layouts: 3 us -> none
    pallas_call x1, Pallas kernels: 90.8 us -> 88.1 us  [local(): pl.pallas_call(kernel, out_shape=[jax.ShapeDtypeStruct((32, n), F32) for...]
    pallas_call x0 -> x1, Pallas kernels: none -> 2.14 us  [local(): pl.pallas_call(finish, out_shape=[jax.ShapeDtypeStruct((32, n), F32) for...]
    transpose x2 -> x0, other arithmetic: 1.61 us -> none  [local(): return ((w + step * p).T, (r - step * q).T)]
where the time goes in v2:
time: 91.7 us; the launch traced here: 91.5 us
  Pallas kernels  90.3 us (98%)
  between operations  1.28 us (1%)
    pallas_call x1, Pallas kernels, local(): pl.pallas_call(kernel, out_shape=[jax.ShapeDtypeStruct((32, n), F32) for...  88.1 us
    pallas_call x1, Pallas kernels, local(): pl.pallas_call(finish, out_shape=[jax.ShapeDtypeStruct((32, n), F32) for...  2.14 us

profile of v2, /device:TPU:1, one launch (start us, length us, event | category | flops | bytes accessed | tf_op | source)
XLA Modules:
  0.0 91.5 jit_solution(4349983967481025535)
XLA Ops:
  1.3 88.1 %cgls.1 = (f32[32,4096]{1,0:T(8,128)}, f32[32,4096]{1,0:T(8,128)}, f32[32,256]{1,0:T(8,128)}, f32[32,256]{1,0:T(8,128)}, f32[32,128]{1,0:T(8,128)}) custom-call(bf16[256,4096]{1,0:T(8,128)(2,1)} %a_hbm.1, f32[32,256]{1,0:T(8,128)} %bitcast.4, s32[1]{0:T(128)S(6)} %copy.6.count_hbm, f32[1,32]{1,0:T(1,128)} %bitcast.5), custom_call_target="tpu_custom_call" | custom-call | tf_op jit(solution)/shard_map/cgls/pallas_call | solution.py:281
  89.4 2.1 %finish.1 = (f32[32,4096]{1,0:T(8,128)}, f32[32,256]{1,0:T(8,128)}) custom-call(f32[32,4096]{1,0:T(8,128)} %get-tuple-element.9.w_hbm, f32[32,4096]{1,0:T(8,128)} %get-tuple-element.10.p_hbm, f32[32,256]{1,0:T(8,128)} %get-tuple-element.11.r_hbm, f32[32,256]{1,0:T(8,128)} %get-tuple-element.12.q_hbm, f32[32,128]{1,0:T(8,128)} %get-tuple-element.13.alpha_hbm), custom_call_target="tpu_custom_call" | custom-call | tf_op jit(solution)/shard_map/finish/pallas_call | solution.py:318

commit v3 on v2

--- a/solution.py
+++ b/solution.py
@@ -20,13 +20,14 @@
 OFFSETS = sorted(((dy, dz) for dy in range(NY) for dz in range(NZ)), key=lambda o: (-hops(o), o))
 PEERS = CHIPS - 1
 GROUPS = ((0, 1), (1, 5), (5, 12), (12, 20), (20, 27), (27, 32))
+LATE = 2
 TILE = 128
 
 
-def kernel(a_hbm, y_hbm, count_hbm, ridge_hbm, w_out, p_out, r_out, q_out, alpha_out,
-           y_ref, count_ref, ridge_ref, in_sems, a, at, ysend, yrecv, mask, r, q, s, p, w, total, tsend, trecv, drow, ahead, g, xbuf, alpha_buf,
+def kernel(a_hbm, y_hbm, count_hbm, ridge_hbm, w_out, r_out,
+           y_ref, count_ref, ridge_ref, in_sems, a, at, ysend, yrecv, mask, r, q, s, p, w, total, tsend, trecv, drow, ahead, g, xbuf, dlast, state_out, state_in, w2, p2, r2, q2,
            load_sem, push_send, push_recv, y_sems, t_send, t_recv, d_send, d_recv,
-           g_send, g_recv, x_send, x_recv, pub_local, pub_send, pub_recv):
+           g_send, g_recv, x_send, x_recv, dl_send, dl_recv, pub_local, pub_send, pub_recv):
     tok, x = lax.axis_index("tok"), lax.axis_index("feat")
     core = lax.rem(tok, 2)
     z, y = lax.rem(tok // 2, NZ), tok // (2 * NZ)
@@ -36,6 +37,7 @@
     others = pl.ds(pl.multiple_of((1 - core) * 256, 256), 256)
     sibling = (me * 2 + 1 - core, x)
     peers = [(chip * 2 + core, x) for chip in chips[:PEERS]]
+    cross_peers = [(chip * 2 + 1 - core, x) for chip in chips[:PEERS]]
     x_peers = [(tok, lax.rem(x + d, NX)) for d in (2, 1, 3)]
 
     def tile(chip):
@@ -55,7 +57,7 @@
         pltpu.make_async_copy(ref, ref, sem).wait()
 
     barrier = pltpu.get_barrier_semaphore()
-    for device in peers + x_peers + [sibling]:
+    for device in peers + x_peers + [sibling] + cross_peers:
         pl.semaphore_signal(barrier, inc=1, device_id=device, device_id_type=MESH)
 
     inputs = [
@@ -86,9 +88,12 @@
     sub = lax.broadcasted_iota(jnp.int32, (16, TILE), 0)
     eye = (lane == sub).astype(F32)
     field = lane // 16
-    pick = (lax.broadcasted_iota(jnp.int32, (16, 32), 1)
-            == lax.broadcasted_iota(jnp.int32, (16, 32), 0) + core * 16).astype(F32)
-    ridge = jnp.sum(ridge_ref[...] * pick, axis=1, keepdims=True)
+    def ridge_of(which):
+        pick = (lax.broadcasted_iota(jnp.int32, (16, 32), 1)
+                == lax.broadcasted_iota(jnp.int32, (16, 32), 0) + which * 16).astype(F32)
+        return jnp.sum(ridge_ref[...] * pick, axis=1, keepdims=True)
+
+    ridge, ridge2 = ridge_of(core), ridge_of(1 - core)
 
     def to_row(column, which):
         return jnp.sum(column * which, axis=0, keepdims=True)
@@ -121,10 +126,16 @@
             row = row + drow[n, j]
         return to_column(row, eye)
 
+    def last_curvature(which):
+        row = dlast[which * CHIPS]
+        for j in range(1, CHIPS):
+            row = row + dlast[which * CHIPS + j]
+        return to_column(row, eye)
+
     def send_row(n, j):
         send(drow.at[n, me], drow.at[n, me], d_send, d_recv.at[n], peers[j])
 
-    pl.semaphore_wait(barrier, PEERS + NX)
+    pl.semaphore_wait(barrier, 2 * PEERS + NX)
 
     y_copy = send(ysend, yrecv, y_sems.at[0], y_sems.at[1], sibling)
     pushes = []
@@ -184,9 +195,11 @@
         total[...] = (1.0 - ratio) * total[...]
 
         image = jnp.zeros((16, 512), F32)
-        for group, (lo, hi) in reversed(list(enumerate(GROUPS))):
-            wait(ahead.at[n, :, slots(0, min(hi, PEERS) - lo)], g_recv.at[n, group])
-            for j in reversed(range(lo, hi)):
+        for last in (LATE, *range(LATE + 1, len(GROUPS)))[::-1]:
+            for group in range(LATE, -1, -1) if last == LATE else (last,):
+                lo, hi = GROUPS[group]
+                wait(ahead.at[n, :, slots(0, min(hi, PEERS) - lo)], g_recv.at[n, group])
+            for j in reversed(range(0 if last == LATE else lo, GROUPS[last][1])):
                 at_j = tile(chips[j])
                 grad = total[:, at_j] + ratio * ahead[n, :, at_j].astype(F32)
                 total[:, at_j] = grad
@@ -215,60 +228,54 @@
     gamma, norm, guess, beta = lax.fori_loop(0, ITERS, step, (one, one, one, one))
 
     for j in range(PEERS):
-        send_row(ITERS, j)
-
-    def publish(k, here, there, out):
-        pltpu.make_async_copy(here, out.at[own_rows], pub_local.at[k]).start()
-        send(there, out.at[own_rows], pub_send.at[k], pub_recv.at[k], sibling)
-
-    publish(0, w, w, w_out)
-    publish(1, r.at[:, mine], r.at[:, others], r_out)
-    publish(2, q.at[:, mine], q.at[:, others], q_out)
+        for device in (peers[j], cross_peers[j]):
+            send(drow.at[ITERS, me], dlast.at[core * CHIPS + me], dl_send, dl_recv, device)
+    send(drow.at[ITERS, me], dlast.at[core * CHIPS + me], dl_send, dl_recv, sibling)
+    dlast[core * CHIPS + me] = drow[ITERS, me]
+    state_out[0] = jnp.broadcast_to(gamma, (16, TILE))
+    state_out[1] = jnp.broadcast_to(norm, (16, TILE))
+    send(state_out, state_in, pub_send.at[0], pub_recv.at[0], sibling)
+    send(w, w2, pub_send.at[1], pub_recv.at[1], sibling)
+    send(r.at[:, others], r2, pub_send.at[2], pub_recv.at[2], sibling)
+    send(q.at[:, others], q2, pub_send.at[3], pub_recv.at[3], sibling)
     p[...] = g[...].astype(F32) + beta * p[...]
-    publish(3, p, p, p_out)
-    alpha = gamma / (curvature(ITERS) + ridge * norm)
-    alpha_buf[...] = jnp.broadcast_to(alpha, alpha_buf.shape)
-    publish(4, alpha_buf, alpha_buf, alpha_out)
-    for k, (src, out) in enumerate(((w, w_out), (r.at[:, mine], r_out), (q.at[:, mine], q_out),
-                                    (p, p_out), (alpha_buf, alpha_out))):
-        wait(src, pub_local.at[k])
-        wait(src, pub_send.at[k])
-        wait(out.at[sibling_rows], pub_recv.at[k])
+    send(p, p2, pub_send.at[4], pub_recv.at[4], sibling)
+    for k, ref in enumerate((state_in, w2, r2, q2, p2)):
+        wait(ref, pub_recv.at[k])
+        wait(ref, pub_send.at[k])
+    wait(dlast.at[pl.ds(0, 2 * CHIPS - 1)], dl_recv)
+    alpha = gamma / (last_curvature(core) + ridge * norm)
+    alpha2 = state_in[0, :, 0:1] / (last_curvature(1 - core) + ridge2 * state_in[1, :, 0:1])
+    w[...] = w[...] + alpha * p[...]
+    w2[...] = w2[...] + alpha2 * p2[...]
+    r[:, mine] = r[:, mine] - alpha * q[:, mine]
+    r2[...] = r2[...] - alpha2 * q2[...]
+    outs = [pltpu.make_async_copy(src, dst, pub_local.at[k]) for k, (src, dst) in enumerate((
+        (w, w_out.at[own_rows]), (w2, w_out.at[sibling_rows]),
+        (r.at[:, mine], r_out.at[own_rows]), (r2, r_out.at[sibling_rows])))]
+    for copy in outs:
+        copy.start()
+    for copy in outs:
+        copy.wait()
     for push in pushes:
         push.wait_send()
     wait(tsend.at[:, :, slots(0, PEERS)], t_send)
     wait(ahead.at[:, :, slots(0, PEERS)], g_send)
-    wait(drow.at[:, pl.ds(0, PEERS)], d_send)
+    wait(drow.at[pl.ds(0, ITERS), pl.ds(0, PEERS)], d_send)
+    wait(dlast.at[pl.ds(0, 2 * CHIPS - 1)], dl_send)
     wait(xbuf.at[:, pl.ds(0, NX - 1)], x_send)
 
 
-PARTS = 4
-
-
-def finish(w_hbm, p_hbm, r_hbm, q_hbm, alpha_hbm, w_out, r_out, w, p, r, q, alpha, in_sems, out_sems):
-    width = w.shape[1] // PARTS
-    parts = [(slice(None), slice(k * width, (k + 1) * width)) for k in range(PARTS)]
-    small = [
-        pltpu.make_async_copy(src, dst, in_sems.at[k])
-        for k, (src, dst) in enumerate(((alpha_hbm, alpha), (r_hbm, r), (q_hbm, q)))]
-    large = [
-        pltpu.make_async_copy(src.at[part], dst.at[part], in_sems.at[3 + 2 * k + which])
-        for k, part in enumerate(parts) for which, (src, dst) in enumerate(((w_hbm, w), (p_hbm, p)))]
-    for copy in small + large:
-        copy.start()
-    for copy in small:
-        copy.wait()
-    step = alpha[:, 0:1]
-    r[...] = r[...] - step * q[...]
-    stores = [pltpu.make_async_copy(r, r_out, out_sems.at[PARTS])]
-    stores[0].start()
-    for k, part in enumerate(parts):
-        large[2 * k].wait()
-        large[2 * k + 1].wait()
-        w[part] = w[part] + step * p[part]
-        store = pltpu.make_async_copy(w.at[part], w_out.at[part], out_sems.at[k])
+def hand_over(w_in, r_in, w_out, r_out, w, r, sems):
+    parts = [(r_in, r, r_out)] + [
+        (w_in.at[rows], w.at[rows], w_out.at[rows]) for rows in (pl.ds(8 * k, 8) for k in range(4))]
+    loads = [pltpu.make_async_copy(src, at, sems.at[0, k]) for k, (src, at, _) in enumerate(parts)]
+    stores = [pltpu.make_async_copy(at, dst, sems.at[1, k]) for k, (_, at, dst) in enumerate(parts)]
+    for load in loads:
+        load.start()
+    for load, store in zip(loads, stores):
+        load.wait()
         store.start()
-        stores.append(store)
     for store in stores:
         store.wait()
 
@@ -278,11 +285,11 @@
     hbm = pl.BlockSpec(memory_space=pltpu.HBM)
     dma = pltpu.SemaphoreType.DMA
     groups = len(GROUPS)
-    w, p, r, q, alpha = pl.pallas_call(
+    w, r = pl.pallas_call(
         kernel,
-        out_shape=[jax.ShapeDtypeStruct((32, n), F32) for n in (4096, 4096, 256, 256, TILE)],
+        out_shape=[jax.ShapeDtypeStruct((32, n), F32) for n in (4096, 256)],
         in_specs=[hbm] * 4,
-        out_specs=[any_] * 5,
+        out_specs=[any_] * 2,
         scratch_shapes=[
             pltpu.VMEM((32, 256), F32),
             pltpu.SMEM((1,), jnp.int32),
@@ -305,10 +312,16 @@
             pltpu.VMEM((ITERS, 16, 4096), BF16),
             pltpu.VMEM((16, 4096), BF16),
             pltpu.VMEM((ITERS, NX, 16, 512 + TILE), BF16),
-            pltpu.VMEM((16, TILE), F32),
+            pltpu.VMEM((2 * CHIPS, 1, TILE), F32),
+            pltpu.VMEM((2, 16, TILE), F32),
+            pltpu.VMEM((2, 16, TILE), F32),
+            pltpu.VMEM((16, 4096), F32),
+            pltpu.VMEM((16, 4096), F32),
+            pltpu.VMEM((16, 256), F32),
+            pltpu.VMEM((16, 256), F32),
             dma((groups,)), dma((groups,)), dma((groups,)), dma((2,)),
             dma, dma((ITERS, groups)), dma, dma((ITERS + 1,)),
-            dma, dma((ITERS, groups)), dma, dma((ITERS,)),
+            dma, dma((ITERS, groups)), dma, dma((ITERS,)), dma, dma,
             dma((5,)), dma((5,)), dma((5,)),
         ],
         compiler_params=pltpu.CompilerParams(
@@ -316,18 +329,14 @@
         name="cgls",
     )(activations, targets.T, counts, ridge[None, :])
     w, r = pl.pallas_call(
-        finish,
+        hand_over,
         out_shape=[jax.ShapeDtypeStruct((32, n), F32) for n in (4096, 256)],
-        in_specs=[hbm] * 5,
+        in_specs=[hbm] * 2,
         out_specs=[any_] * 2,
-        scratch_shapes=[
-            pltpu.VMEM((32, 4096), F32), pltpu.VMEM((32, 4096), F32),
-            pltpu.VMEM((32, 256), F32), pltpu.VMEM((32, 256), F32), pltpu.VMEM((32, TILE), F32),
-            dma((2 * PARTS + 3,)), dma((PARTS + 1,)),
-        ],
+        scratch_shapes=[pltpu.VMEM((32, 4096), F32), pltpu.VMEM((32, 256), F32), dma((2, 5))],
         compiler_params=pltpu.CompilerParams(vmem_limit_bytes=58 * 2**20),
-        name="finish",
-    )(w, p, r, q, alpha)
+        name="hand_over",
+    )(w, r)
     return w.T, r.T
 
 

time: 91.7 us -> 91 us (level)
  no operation moved by 1% of the time
where the time goes in v3:
time: 91 us; the launch traced here: 90.8 us
  Pallas kernels  89.5 us (98%)
  between operations  1.28 us (1%)
    pallas_call x1, Pallas kernels, local(): pl.pallas_call(kernel, out_shape=[jax.ShapeDtypeStruct((32, n), F32) for...  87.7 us
    pallas_call x1, Pallas kernels, local(): pl.pallas_call(hand_over, out_shape=[jax.ShapeDtypeStruct((32, n), F32) f...  1.86 us

profile of v3, /device:TPU:1, one launch (start us, length us, event | category | flops | bytes accessed | tf_op | source)
XLA Modules:
  0.0 90.8 jit_solution(10839657205533022337)
XLA Ops:
  1.3 87.7 %cgls.1 = (f32[32,4096]{1,0:T(8,128)}, f32[32,256]{1,0:T(8,128)}) custom-call(bf16[256,4096]{1,0:T(8,128)(2,1)} %a_hbm.1, f32[32,256]{1,0:T(8,128)} %bitcast.4, s32[1]{0:T(128)S(6)} %copy.6.count_hbm, f32[1,32]{1,0:T(1,128)} %bitcast.5), custom_call_target="tpu_custom_call" | custom-call | tf_op jit(solution)/shard_map/cgls/pallas_call | solution.py:288
  89.0 1.9 %hand_over.1 = (f32[32,4096]{1,0:T(8,128)}, f32[32,256]{1,0:T(8,128)}) custom-call(f32[32,4096]{1,0:T(8,128)} %get-tuple-element.6.w_in, f32[32,256]{1,0:T(8,128)} %get-tuple-element.7.r_in), custom_call_target="tpu_custom_call" | custom-call | tf_op jit(solution)/shard_map/hand_over/pallas_call | solution.py:331

commit v4 on v3

--- a/solution.py
+++ b/solution.py
@@ -21,12 +21,14 @@
 PEERS = CHIPS - 1
 GROUPS = ((0, 1), (1, 5), (5, 12), (12, 20), (20, 27), (27, 32))
 LATE = 2
+FAR_GROUPS = 2
+FAR = GROUPS[FAR_GROUPS - 1][1]
 TILE = 128
 
 
 def kernel(a_hbm, y_hbm, count_hbm, ridge_hbm, w_out, r_out,
-           y_ref, count_ref, ridge_ref, in_sems, a, at, ysend, yrecv, mask, r, q, s, p, w, total, tsend, trecv, drow, ahead, g, xbuf, dlast, state_out, state_in, w2, p2, r2, q2,
-           load_sem, push_send, push_recv, y_sems, t_send, t_recv, d_send, d_recv,
+           y_ref, count_ref, ridge_ref, in_sems, a, at, ysend, yrecv, mask, r, q, s, p, w, total, tsend, trecv, fsend, fextra, drow, ahead, g, xbuf, dlast, state_out, state_in, w2, p2, r2, q2,
+           load_sem, push_send, push_recv, y_sems, t_send, t_recv, f_send, f_recv, d_send, d_recv,
            g_send, g_recv, x_send, x_recv, dl_send, dl_recv, pub_local, pub_send, pub_recv):
     tok, x = lax.axis_index("tok"), lax.axis_index("feat")
     core = lax.rem(tok, 2)
@@ -135,39 +137,63 @@
     def send_row(n, j):
         send(drow.at[n, me], drow.at[n, me], d_send, d_recv.at[n], peers[j])
 
+    for group in range(FAR_GROUPS):
+        wait(a.at[mine, slots(*GROUPS[group])], load_sem.at[group])
+    for k, rows in enumerate((r[:, mine], ysend[0:16, :])):
+        fsend[k] = jnp.dot(rows.astype(BF16), a[mine, slots(0, FAR)], preferred_element_type=F32).astype(BF16)
+
     pl.semaphore_wait(barrier, 2 * PEERS + NX)
 
+    for group in range(FAR_GROUPS):
+        for j in range(*GROUPS[group]):
+            send(fsend.at[0, :, slots(j, j + 1)], trecv.at[0, j], t_send, t_recv.at[0, group], peers[j])
+            send(fsend.at[1, :, slots(j, j + 1)], fextra.at[j], f_send, f_recv, cross_peers[j])
+
     y_copy = send(ysend, yrecv, y_sems.at[0], y_sems.at[1], sibling)
-    pushes = []
-    for group, (lo, hi) in enumerate(GROUPS):
-        wait(a.at[mine, slots(lo, hi)], load_sem.at[group])
-        part = a.at[mine, slots(lo, hi)]
-        pushes.append(send(part, part, push_send.at[group], push_recv.at[group], sibling))
+    pushes = {}
+    for group in (*range(FAR_GROUPS, len(GROUPS)), *range(FAR_GROUPS)):
+        part = a.at[mine, slots(*GROUPS[group])]
+        if group >= FAR_GROUPS:
+            wait(part, load_sem.at[group])
+        pushes[group] = send(part, part, push_send.at[group], push_recv.at[group], sibling)
     y_copy.wait()
     r[:, others] = yrecv[0:16, :]
     mask[:, others] = yrecv[16:24, :]
     s[...] = r[...].astype(BF16)
-    drow[0, me] = to_row(lanes(r[...] * r[...]), eye)
 
     def step(n, carry):
         gamma, norm, guess, beta = carry
         first = n == 0
         inv_gamma, inv_guess = 1.0 / gamma, 1.0 / guess
-        for group, (lo, hi) in enumerate(GROUPS):
-            @pl.when(n == 0)
-            def _():
-                pushes[group].wait_recv()
+        def scatter(group, lo, hi):
             part = jnp.dot(s[...], a[:, slots(lo, hi)], preferred_element_type=F32)
             tsend[n, :, slots(lo, hi)] = part.astype(BF16)
             for j in range(lo, min(hi, PEERS)):
                 send(tsend.at[n, :, slots(j, j + 1)], trecv.at[n, j], t_send, t_recv.at[n, group], peers[j])
+            return part
+
+        for group, (lo, hi) in enumerate(GROUPS):
+            if group < FAR_GROUPS:
+                @pl.when(n > 0)
+                def _():
+                    scatter(group, lo, hi)
+                continue
+
+            @pl.when(n == 0)
+            def _():
+                pushes[group].wait_recv()
+            part = scatter(group, lo, hi)
             if hi == CHIPS:
                 summed = part[:, (PEERS - lo) * TILE:]
+        rows = jnp.where(first, r[...], q[...])
+        drow[n, me] = to_row(lanes(rows * rows), eye)
         for j in range(PEERS):
             send_row(n, j)
 
         @pl.when(n == 0)
         def _():
+            for group in range(FAR_GROUPS):
+                pushes[group].wait_recv()
             for lo, hi in GROUPS:
                 at[slots(lo, hi), :] = a[:, slots(lo, hi)].T
 
@@ -181,6 +207,13 @@
             wait(trecv.at[n, pl.ds(lo, hi - lo)], t_recv.at[n, group])
             for j in range(lo, hi):
                 summed = summed + trecv[n, j].astype(F32)
+        @pl.when(n == 0)
+        def _():
+            wait(fextra, f_recv)
+        extra = fextra[0].astype(F32)
+        for j in range(1, FAR):
+            extra = extra + fextra[j].astype(F32)
+        summed = summed + jnp.where(first, extra, 0.0)
         ahead[n, :, tile(me)] = summed.astype(BF16)
         for group, (lo, hi) in enumerate(GROUPS):
             for j in range(lo, min(hi, PEERS)):
@@ -192,7 +225,7 @@
         ratio = jnp.where(first, 1.0, alpha * inv_guess)
         r[...] = r[...] - alpha * q[...]
         w[...] = w[...] + alpha * p[...]
-        total[...] = (1.0 - ratio) * total[...]
+        keep = 1.0 - ratio
 
         image = jnp.zeros((16, 512), F32)
         for last in (LATE, *range(LATE + 1, len(GROUPS)))[::-1]:
@@ -201,7 +234,7 @@
                 wait(ahead.at[n, :, slots(0, min(hi, PEERS) - lo)], g_recv.at[n, group])
             for j in reversed(range(0 if last == LATE else lo, GROUPS[last][1])):
                 at_j = tile(chips[j])
-                grad = total[:, at_j] + ratio * ahead[n, :, at_j].astype(F32)
+                grad = keep * total[:, at_j] + ratio * ahead[n, :, at_j].astype(F32)
                 total[:, at_j] = grad
                 grad = grad.astype(BF16)
                 g[:, at_j] = grad
@@ -221,12 +254,12 @@
         fresh_q = image[:, 0:512] * mask[0:1, :] + beta * q[...]
         q[...] = fresh_q
         s[...] = (r[...] - guess * fresh_q).astype(BF16)
-        drow[n + 1, me] = to_row(lanes(fresh_q * fresh_q), eye)
         return gamma_new, norm, guess, beta
 
     one = jnp.ones((16, 1), F32)
     gamma, norm, guess, beta = lax.fori_loop(0, ITERS, step, (one, one, one, one))
 
+    drow[ITERS, me] = to_row(lanes(q[...] * q[...]), eye)
     for j in range(PEERS):
         for device in (peers[j], cross_peers[j]):
             send(drow.at[ITERS, me], dlast.at[core * CHIPS + me], dl_send, dl_recv, device)
@@ -257,8 +290,9 @@
         copy.start()
     for copy in outs:
         copy.wait()
-    for push in pushes:
+    for push in pushes.values():
         push.wait_send()
+    wait(fextra, f_send)
     wait(tsend.at[:, :, slots(0, PEERS)], t_send)
     wait(ahead.at[:, :, slots(0, PEERS)], g_send)
     wait(drow.at[pl.ds(0, ITERS), pl.ds(0, PEERS)], d_send)
@@ -308,6 +342,8 @@
             pltpu.VMEM((16, 4096), F32),
             pltpu.VMEM((ITERS, 16, 4096), BF16),
             pltpu.VMEM((ITERS, PEERS, 16, TILE), BF16),
+            pltpu.VMEM((2, 16, FAR * TILE), BF16),
+            pltpu.VMEM((FAR, 16, TILE), BF16),
             pltpu.VMEM((ITERS + 1, CHIPS, 1, TILE), F32),
             pltpu.VMEM((ITERS, 16, 4096), BF16),
             pltpu.VMEM((16, 4096), BF16),
@@ -320,7 +356,7 @@
             pltpu.VMEM((16, 256), F32),
             pltpu.VMEM((16, 256), F32),
             dma((groups,)), dma((groups,)), dma((groups,)), dma((2,)),
-            dma, dma((ITERS, groups)), dma, dma((ITERS + 1,)),
+            dma, dma((ITERS, groups)), dma, dma, dma, dma((ITERS + 1,)),
             dma, dma((ITERS, groups)), dma, dma((ITERS,)), dma, dma,
             dma((5,)), dma((5,)), dma((5,)),
         ],

time: 91 us -> 89.6 us (0.985)
  Pallas kernels: 89.5 us -> 88.1 us
    pallas_call x1, Pallas kernels: 87.7 us -> 86.2 us  [local(): pl.pallas_call(kernel, out_shape=[jax.ShapeDtypeStruct((32, n), F32) for...]
where the time goes in v4:
time: 89.6 us; the launch traced here: 89.4 us
  Pallas kernels  88.1 us (98%)
  between operations  1.28 us (1%)
    pallas_call x1, Pallas kernels, local(): pl.pallas_call(kernel, out_shape=[jax.ShapeDtypeStruct((32, n), F32) for...  86.2 us
    pallas_call x1, Pallas kernels, local(): pl.pallas_call(hand_over, out_shape=[jax.ShapeDtypeStruct((32, n), F32) f...  1.86 us

profile of v4, /device:TPU:1, one launch (start us, length us, event | category | flops | bytes accessed | tf_op | source)
XLA Modules:
  0.0 89.4 jit_solution(3474442332224705273)
XLA Ops:
  1.3 86.2 %cgls.1 = (f32[32,4096]{1,0:T(8,128)}, f32[32,256]{1,0:T(8,128)}) custom-call(bf16[256,4096]{1,0:T(8,128)(2,1)} %a_hbm.1, f32[32,256]{1,0:T(8,128)} %bitcast.4, s32[1]{0:T(128)S(6)} %copy.6.count_hbm, f32[1,32]{1,0:T(1,128)} %bitcast.5), custom_call_target="tpu_custom_call" | custom-call | tf_op jit(solution)/shard_map/cgls/pallas_call | solution.py:322
  87.5 1.9 %hand_over.1 = (f32[32,4096]{1,0:T(8,128)}, f32[32,256]{1,0:T(8,128)}) custom-call(f32[32,4096]{1,0:T(8,128)} %get-tuple-element.6.w_in, f32[32,256]{1,0:T(8,128)} %get-tuple-element.7.r_in), custom_call_target="tpu_custom_call" | custom-call | tf_op jit(solution)/shard_map/hand_over/pallas_call | solution.py:367

commit v5 on v4

--- a/solution.py
+++ b/solution.py
@@ -17,13 +17,19 @@
     return min(dy, NY - dy) + min(dz, NZ - dz)
 
 
-OFFSETS = sorted(((dy, dz) for dy in range(NY) for dz in range(NZ)), key=lambda o: (-hops(o), o))
+OFFSETS = sorted(((dy, dz) for dy in range(NY) for dz in range(NZ)), key=lambda o: (-hops(o), min(o[1], NZ - o[1]), o))
 PEERS = CHIPS - 1
 GROUPS = ((0, 1), (1, 5), (5, 12), (12, 20), (20, 27), (27, 32))
-LATE = 2
+LATE = 1
 FAR_GROUPS = 2
 FAR = GROUPS[FAR_GROUPS - 1][1]
 TILE = 128
+
+
+def add_up(parts):
+    while len(parts) > 1:
+        parts = [sum(parts[i + 1:i + 2], parts[i]) for i in range(0, len(parts), 2)]
+    return parts[0]
 
 
 def kernel(a_hbm, y_hbm, count_hbm, ridge_hbm, w_out, r_out,
@@ -104,9 +110,7 @@
         return jnp.sum(row * which, axis=1, keepdims=True)
 
     def lanes(v):
-        out = v[:, 0:TILE]
-        for j in range(1, v.shape[1] // TILE):
-            out = out + v[:, j * TILE:(j + 1) * TILE]
+        out = add_up([v[:, j:j + TILE] for j in range(0, v.shape[1], TILE)])
         return jnp.sum(out, axis=1, keepdims=True)
 
     def pack(*columns):
@@ -123,16 +127,10 @@
 
     def curvature(n):
         wait(drow.at[n, pl.ds(0, PEERS)], d_recv.at[n])
-        row = drow[n, 0]
-        for j in range(1, CHIPS):
-            row = row + drow[n, j]
-        return to_column(row, eye)
+        return to_column(add_up([drow[n, j] for j in range(CHIPS)]), eye)
 
     def last_curvature(which):
-        row = dlast[which * CHIPS]
-        for j in range(1, CHIPS):
-            row = row + dlast[which * CHIPS + j]
-        return to_column(row, eye)
+        return to_column(add_up([dlast[which * CHIPS + j] for j in range(CHIPS)]), eye)
 
     def send_row(n, j):
         send(drow.at[n, me], drow.at[n, me], d_send, d_recv.at[n], peers[j])

time: 89.6 us -> 88.7 us (0.990)
  no operation moved by 1% of the time
where the time goes in v5:
time: 88.7 us; the launch traced here: 88.6 us
  Pallas kernels  87.3 us (98%)
  between operations  1.28 us (1%)
    pallas_call x1, Pallas kernels, local(): pl.pallas_call(kernel, out_shape=[jax.ShapeDtypeStruct((32, n), F32) for...  85.4 us
    pallas_call x1, Pallas kernels, local(): pl.pallas_call(hand_over, out_shape=[jax.ShapeDtypeStruct((32, n), F32) f...  1.86 us

profile of v5, /device:TPU:1, one launch (start us, length us, event | category | flops | bytes accessed | tf_op | source)
XLA Modules:
  0.0 88.6 jit_solution(6067470254335894870)
XLA Ops:
  1.3 85.4 %cgls.1 = (f32[32,4096]{1,0:T(8,128)}, f32[32,256]{1,0:T(8,128)}) custom-call(bf16[256,4096]{1,0:T(8,128)(2,1)} %a_hbm.1, f32[32,256]{1,0:T(8,128)} %bitcast.4, s32[1]{0:T(128)S(6)} %copy.6.count_hbm, f32[1,32]{1,0:T(1,128)} %bitcast.5), custom_call_target="tpu_custom_call" | custom-call | tf_op jit(solution)/shard_map/cgls/pallas_call | solution.py:320
  86.7 1.9 %hand_over.1 = (f32[32,4096]{1,0:T(8,128)}, f32[32,256]{1,0:T(8,128)}) custom-call(f32[32,4096]{1,0:T(8,128)} %get-tuple-element.6.w_in, f32[32,256]{1,0:T(8,128)} %get-tuple-element.7.r_in), custom_call_target="tpu_custom_call" | custom-call | tf_op jit(solution)/shard_map/hand_over/pallas_call | solution.py:365

commit v6 on v5

--- a/solution.py
+++ b/solution.py
@@ -160,7 +160,7 @@
     s[...] = r[...].astype(BF16)
 
     def step(n, carry):
-        gamma, norm, guess, beta = carry
+        gamma, norm, guess, beta, alpha = carry
         first = n == 0
         inv_gamma, inv_guess = 1.0 / gamma, 1.0 / guess
         def scatter(group, lo, hi):
@@ -197,21 +197,21 @@
 
         @pl.when(n > 0)
         def _():
+            w[...] = w[...] + alpha * p[...]
             p[...] = g[...].astype(F32) + beta * p[...]
 
         summed = summed - ridge * (w[:, tile(me)] + guess * p[:, tile(me)])
         for group, (lo, hi) in reversed(list(enumerate(GROUPS))):
             hi = min(hi, PEERS)
+            if group == 0:
+                @pl.when(n == 0)
+                def _():
+                    wait(fextra, f_recv)
+                extra = add_up([fextra[j].astype(F32) for j in range(FAR)])
+                summed = summed + jnp.where(first, extra, 0.0)
             wait(trecv.at[n, pl.ds(lo, hi - lo)], t_recv.at[n, group])
             for j in range(lo, hi):
                 summed = summed + trecv[n, j].astype(F32)
-        @pl.when(n == 0)
-        def _():
-            wait(fextra, f_recv)
-        extra = fextra[0].astype(F32)
-        for j in range(1, FAR):
-            extra = extra + fextra[j].astype(F32)
-        summed = summed + jnp.where(first, extra, 0.0)
         ahead[n, :, tile(me)] = summed.astype(BF16)
         for group, (lo, hi) in enumerate(GROUPS):
             for j in range(lo, min(hi, PEERS)):
@@ -222,7 +222,6 @@
         alpha = jnp.where(first, 0.0, gamma / (energy + ridge * norm))
         ratio = jnp.where(first, 1.0, alpha * inv_guess)
         r[...] = r[...] - alpha * q[...]
-        w[...] = w[...] + alpha * p[...]
         keep = 1.0 - ratio
 
         image = jnp.zeros((16, 512), F32)
@@ -252,10 +251,10 @@
         fresh_q = image[:, 0:512] * mask[0:1, :] + beta * q[...]
         q[...] = fresh_q
         s[...] = (r[...] - guess * fresh_q).astype(BF16)
-        return gamma_new, norm, guess, beta
+        return gamma_new, norm, guess, beta, alpha
 
     one = jnp.ones((16, 1), F32)
-    gamma, norm, guess, beta = lax.fori_loop(0, ITERS, step, (one, one, one, one))
+    gamma, norm, guess, beta, alpha = lax.fori_loop(0, ITERS, step, (one,) * 5)
 
     drow[ITERS, me] = to_row(lanes(q[...] * q[...]), eye)
     for j in range(PEERS):
@@ -266,6 +265,7 @@
     state_out[0] = jnp.broadcast_to(gamma, (16, TILE))
     state_out[1] = jnp.broadcast_to(norm, (16, TILE))
     send(state_out, state_in, pub_send.at[0], pub_recv.at[0], sibling)
+    w[...] = w[...] + alpha * p[...]
     send(w, w2, pub_send.at[1], pub_recv.at[1], sibling)
     send(r.at[:, others], r2, pub_send.at[2], pub_recv.at[2], sibling)
     send(q.at[:, others], q2, pub_send.at[3], pub_recv.at[3], sibling)

time: 88.7 us -> 88.6 us (level)
  no operation moved by 1% of the time
where the time goes in v6:
time: 88.6 us; the launch traced here: 88.4 us
  Pallas kernels  87.2 us (98%)
  between operations  1.28 us (1%)
    pallas_call x1, Pallas kernels, local(): pl.pallas_call(kernel, out_shape=[jax.ShapeDtypeStruct((32, n), F32) for...  85.3 us
    pallas_call x1, Pallas kernels, local(): pl.pallas_call(hand_over, out_shape=[jax.ShapeDtypeStruct((32, n), F32) f...  1.86 us

profile of v6, /device:TPU:1, one launch (start us, length us, event | category | flops | bytes accessed | tf_op | source)
XLA Modules:
  0.0 88.4 jit_solution(5281675006778469591)
XLA Ops:
  1.3 85.3 %cgls.1 = (f32[32,4096]{1,0:T(8,128)}, f32[32,256]{1,0:T(8,128)}) custom-call(bf16[256,4096]{1,0:T(8,128)(2,1)} %a_hbm.1, f32[32,256]{1,0:T(8,128)} %bitcast.4, s32[1]{0:T(128)S(6)} %copy.6.count_hbm, f32[1,32]{1,0:T(1,128)} %bitcast.5), custom_call_target="tpu_custom_call" | custom-call | tf_op jit(solution)/shard_map/cgls/pallas_call | solution.py:320
  86.6 1.9 %hand_over.1 = (f32[32,4096]{1,0:T(8,128)}, f32[32,256]{1,0:T(8,128)}) custom-call(f32[32,4096]{1,0:T(8,128)} %get-tuple-element.6.w_in, f32[32,256]{1,0:T(8,128)} %get-tuple-element.7.r_in), custom_call_target="tpu_custom_call" | custom-call | tf_op jit(solution)/shard_map/hand_over/pallas_call | solution.py:365

commit v7 on v6

--- a/solution.py
+++ b/solution.py
@@ -20,7 +20,7 @@
 OFFSETS = sorted(((dy, dz) for dy in range(NY) for dz in range(NZ)), key=lambda o: (-hops(o), min(o[1], NZ - o[1]), o))
 PEERS = CHIPS - 1
 GROUPS = ((0, 1), (1, 5), (5, 12), (12, 20), (20, 27), (27, 32))
-LATE = 1
+LATE = 0
 FAR_GROUPS = 2
 FAR = GROUPS[FAR_GROUPS - 1][1]
 TILE = 128

time: 88.6 us -> 89.2 us (level)
  no operation moved by 1% of the time
where the time goes in v7:
time: 89.2 us; the launch traced here: 89.1 us
  Pallas kernels  87.8 us (98%)
  between operations  1.28 us (1%)
    pallas_call x1, Pallas kernels, local(): pl.pallas_call(kernel, out_shape=[jax.ShapeDtypeStruct((32, n), F32) for...  85.9 us
    pallas_call x1, Pallas kernels, local(): pl.pallas_call(hand_over, out_shape=[jax.ShapeDtypeStruct((32, n), F32) f...  1.86 us

profile of v7, /device:TPU:1, one launch (start us, length us, event | category | flops | bytes accessed | tf_op | source)
XLA Modules:
  0.0 89.1 jit_solution(8191975785343573644)
XLA Ops:
  1.3 85.9 %cgls.1 = (f32[32,4096]{1,0:T(8,128)}, f32[32,256]{1,0:T(8,128)}) custom-call(bf16[256,4096]{1,0:T(8,128)(2,1)} %a_hbm.1, f32[32,256]{1,0:T(8,128)} %bitcast.4, s32[1]{0:T(128)S(6)} %copy.6.count_hbm, f32[1,32]{1,0:T(1,128)} %bitcast.5), custom_call_target="tpu_custom_call" | custom-call | tf_op jit(solution)/shard_map/cgls/pallas_call | solution.py:320
  87.2 1.9 %hand_over.1 = (f32[32,4096]{1,0:T(8,128)}, f32[32,256]{1,0:T(8,128)}) custom-call(f32[32,4096]{1,0:T(8,128)} %get-tuple-element.6.w_in, f32[32,256]{1,0:T(8,128)} %get-tuple-element.7.r_in), custom_call_target="tpu_custom_call" | custom-call | tf_op jit(solution)/shard_map/hand_over/pallas_call | solution.py:365
